TPU v7x, 256 devices: a whole 4x4x8 slice. The times are simulated.
256 devices in a mesh: grp: 4 (over x), grid: 64 (over y, z, core).
Axes of the slice: x: 4, y: 4, z: 8, core: 2. Of those that a mesh axis runs over, the one named last changes fastest.
Arguments:
- orbitals: float32 [512, 262144], P('grp', 'grid'), may hold values from -6 to 6
- anchors: int32 [512, 3], replicated, may hold values from 0 to 31
- pair_slots: int32 [256, 4, 2], replicated, may hold values from -1 to 511, as said below
Outputs:
- exchange_term: float32 [512, 262144], P('grp', 'grid')
Inputs may be any that keep to these rules, and one draw needn't show every extreme that they name: `pair_slots`: row k lists the pairs of owner k, the device with index k in the order grp, grid; its first slots hold pairs of two different orbital numbers and its other slots hold -1 in both columns. Exactly 512 slots hold pairs in all, no row holds more than 4, and some row holds exactly 4.
All inputs are finite; a program needn't handle non-finite values.
Results may differ from a plain program's by a relative error of at most 0.0003.
Values sent between devices are 32-bit elements; how exact they have to be, the bound alone decides.
No kernel may reach another device: no remote copies, remote signals or barrier semaphores. Data moves between devices by JAX's collectives and lax.ppermute only.
A program may use at most 128 MiB of HBM per device.

v0:
```python
import jax
import jax.numpy as jnp
from jax import lax
from jax.sharding import PartitionSpec as P

B = 64
PAIR_DEV = 2
ITERS = 3


def shift_field(field, offset, extent):
    plane_size = extent * extent
    padded_x = jnp.pad(field, ((extent, extent), (0, 0)))
    moved = lax.dynamic_slice_in_dim(padded_x, extent - offset[0], extent, 0)
    padded_yz = jnp.pad(moved, ((0, 0), (plane_size, plane_size)))
    linear = offset[1] * extent + offset[2]
    moved = lax.dynamic_slice_in_dim(padded_yz, plane_size - linear, plane_size, 1)
    cells = lax.broadcasted_iota(jnp.int32, (1, plane_size), 1)
    coord_y = cells // extent - offset[1]
    coord_z = cells % extent - offset[2]
    inside = (coord_y >= 0) & (coord_y < extent) & (coord_z >= 0) & (coord_z < extent)
    return jnp.where(inside, moved, jnp.zeros_like(moved))


def operate(field, extent):
    padded_x = jnp.pad(field, ((1, 1), (0, 0)))
    beside = padded_x[2:] + padded_x[:-2]
    padded_y = jnp.pad(field, ((0, 0), (extent, extent)))
    beside = beside + padded_y[:, 2 * extent :] + padded_y[:, : -2 * extent]
    padded_z = jnp.pad(field, ((0, 0), (1, 1)))
    cells = lax.broadcasted_iota(jnp.int32, (1, field.shape[1]), 1) % extent
    upper_z = jnp.where(cells < extent - 1, padded_z[:, 2:], jnp.zeros_like(field))
    lower_z = jnp.where(cells > 0, padded_z[:, :-2], jnp.zeros_like(field))
    return 6.0 * field - beside - upper_z - lower_z


def conjugate(density, extent):
    potential = jnp.zeros_like(density)
    resid = density
    direction = density
    norm_now = jnp.sum(resid * resid)
    for turn in range(ITERS):
        image = operate(direction, extent)
        step_len = norm_now / jnp.sum(direction * image)
        potential = potential + step_len * direction
        resid = resid - step_len * image
        norm_next = jnp.sum(resid * resid)
        direction = resid + norm_next / norm_now * direction
        norm_now = norm_next
    return potential


def pair_terms(field_a, field_b, offset, extent):
    partner = shift_field(field_b, offset, extent)
    density = field_a * partner
    potential = conjugate(density, extent)
    term_a = potential * partner
    term_b = shift_field(potential * field_a, -offset, extent)
    return (term_a, term_b)


def deal_evenly(pair_slots, owner_count, each_owner):
    flat_slots = pair_slots.reshape(-1, 2)
    filled = (flat_slots[:, 0] >= 0).astype(jnp.int32)
    order = jnp.arange(flat_slots.shape[0], dtype=jnp.int32)
    position = jnp.sum(jnp.where(order[None, :] < order[:, None], filled[None, :], 0), axis=1)
    wanted = lax.broadcasted_iota(jnp.int32, (owner_count, each_owner), 1) * owner_count
    wanted = (wanted + lax.broadcasted_iota(jnp.int32, (owner_count, each_owner), 0)).reshape(-1)
    matched = (position[None, :] == wanted[:, None]) & (filled[None, :] == 1)
    picked = jnp.dot(matched.astype(jnp.int32), flat_slots)
    return picked.reshape(owner_count, each_owner, 2)


def body(orbitals, anchors, pair_slots):
    extent = B
    grid_count = lax.axis_size("grid")
    owner_count = lax.axis_size("grp") * grid_count
    group_idx = lax.axis_index("grp")
    place_idx = lax.axis_index("grid")
    assignment = deal_evenly(pair_slots, owner_count, PAIR_DEV)
    filled = assignment[..., 0] >= 0
    safe_ids = jnp.maximum(assignment, 0)
    pieces = lax.all_gather(orbitals, "grp", axis=0, tiled=True)
    group_table = lax.dynamic_slice_in_dim(safe_ids, group_idx * grid_count, grid_count, 0)
    gather_ids = jnp.transpose(group_table, (1, 2, 0))
    outgoing = pieces[gather_ids]
    arrived = lax.all_to_all(outgoing, "grid", split_axis=2, concat_axis=2, tiled=True)
    owner_idx = group_idx * grid_count + place_idx
    own_pairs = safe_ids[owner_idx]
    own_filled = filled[owner_idx]
    offsets = anchors[own_pairs[:, 1]] - anchors[own_pairs[:, 0]]

    def solve_slot(slot_item):
        boxes_pair, offset, flag = slot_item
        term_a, term_b = pair_terms(boxes_pair[0], boxes_pair[1], offset, extent)
        weight_flag = jnp.where(flag, 1.0, 0.0).astype(jnp.float32)
        return jnp.stack([term_a, term_b]) * weight_flag

    terms = lax.map(solve_slot, (arrived, offsets, own_filled))
    returned = lax.all_to_all(terms, "grid", split_axis=2, concat_axis=2, tiled=True)
    flat_terms = returned.reshape(-1, returned.shape[-1])
    summed = jax.ops.segment_sum(flat_terms, gather_ids.reshape(-1), num_segments=anchors.shape[0])
    return lax.psum_scatter(summed, "grp", scatter_dimension=0, tiled=True)


def solution(mesh):
    return jax.shard_map(
        body,
        mesh=mesh,
        in_specs=(P("grp", "grid"), P(), P()),
        out_specs=P("grp", "grid"),
        check_vma=False,
    )
```

profile of v0, /device:TPU:1, one launch (start us, length us, event | category | flops | bytes accessed | tf_op | source)
XLA Modules:
  0.0 504.9 jit_solution(9031635187783980270)
XLA Ops:
  8.8 1.4 broadcast_maximum_fusion
  10.3 88.3 %all-gather.2.cloned.1.call-done = f32[512,4096]{1,0:T(8,128)} async-done(((f32[128,4096]{1,0:T(8,128)}), f32[512,4096]{1,0:T(8,128)}) %all-gather.2.cloned.1.call-update) | async-done | bytes 8388624 | tf_op jit(solution)/shard_map/all_gather | solution.py:83
  98.7 9.0 %gather_fusion = f32[256,4096]{1,0:T(8,128)} fusion(f32[512,4096]{1,0:T(8,128)} %all-gather.2.cloned.1.call-done, s32[1024]{0:T(1024)S(1)} %pad_clamp_fusion.2), kind=kCustom, calls=%fused_computation | custom fusion | bytes 8389632 | tf_op jit(solution)/shard_map/gather | solution.py:86
  107.7 7.4 %copy.23 = f32[2,2,64,4096]{3,1,0,2:T(2,128)} copy(f32[2,2,64,4096]{3,2,1,0:T(8,128)} %bitcast.60) | data formatting | bytes 8388608 | tf_op jit(solution)/shard_map/gather | solution.py:86
  115.0 11.0 %all-to-all-start = ((f32[2,2,64,4096]{3,1,0,2:T(2,128)}), f32[2,2,64,4096]{3,1,0,2:T(2,128)}, u32[]{:S(2)}, u32[]{:S(2)}) async-start(f32[2,2,64,4096]{3,1,0,2:T(2,128)} %copy.23), calls=%async_computation | async-start | bytes 8388608 | tf_op jit(solution)/shard_map/all_to_all | solution.py:87
  128.0 93.9 %all-to-all-done = f32[2,2,64,4096]{3,1,0,2:T(2,128)} async-done(((f32[2,2,64,4096]{3,1,0,2:T(2,128)}), f32[2,2,64,4096]{3,1,0,2:T(2,128)}, u32[]{:S(2)}, u32[]{:S(2)}) %all-to-all-start) | async-done | bytes 4194336 | tf_op jit(solution)/shard_map/all_to_all | solution.py:87
  222.0 77.1 %while.13 = (s32[]{:T(128)}, f32[2,2,64,4096]{3,1,0,2:T(2,128)}, f32[2,2,64,4096]{3,1,0,2:T(2,128)}, s32[2,3]{1,0:T(2,128)S(1)}, pred[2]{0:T(512)(128)(4,1)S(1)}...) while((s32[]{:T(128)}, f32[2,2,64,4096]{3,1,0,2:T(2,128)}, ...), condition=%wide.region_8.9_spmd, body=%wide.region_1.8_spmd.sunk | while | flops 22224920 | bytes 64017664 | solution.py:99
  225.2 4.4 constant_dynamic-slice_fusion.5
  230.3 1.3 fusion.76
  231.6 1.0 fusion.77
  232.6 1.8 multiply_reduce_fusion.9
  238.1 1.8 multiply_reduce_fusion.11
  243.6 1.8 fusion.79
  246.7 3.9 multiply_bitcast_fusion.2
  252.0 1.3 pad_dynamic-slice_fusion.7
  254.5 1.2 fusion.80
  257.5 3.0 copy_dynamic-update-slice_fusion.2
  263.7 4.4 constant_dynamic-slice_fusion.5
  268.9 1.3 fusion.76
  270.1 1.0 fusion.77
  271.1 1.8 multiply_reduce_fusion.9
  276.6 1.8 multiply_reduce_fusion.11
  282.2 1.8 fusion.79
  285.3 3.9 multiply_bitcast_fusion.2
  290.5 1.3 pad_dynamic-slice_fusion.7
  293.1 1.2 fusion.80
  296.1 3.0 copy_dynamic-update-slice_fusion.2
  299.1 6.0 %all-to-all-start.1 = ((f32[2,2,64,4096]{3,1,0,2:T(2,128)}), f32[2,2,64,4096]{3,1,0,2:T(2,128)}, u32[]{:S(2)}, u32[]{:S(2)}) async-start(f32[2,2,64,4096]{3,1,0,2:T(2,128)} %get-tuple-element.107), calls=%async_computation.1 | async-start | bytes 8388608 | tf_op jit(solution)/shard_map/all_to_all | solution.py:100
  305.2 95.8 %all-to-all-done.1 = f32[2,2,64,4096]{3,1,0,2:T(2,128)} async-done(((f32[2,2,64,4096]{3,1,0,2:T(2,128)}), f32[2,2,64,4096]{3,1,0,2:T(2,128)}, u32[]{:S(2)}, u32[]{:S(2)}) %all-to-all-start.1) | async-done | bytes 4194336 | tf_op jit(solution)/shard_map/all_to_all | solution.py:100
  401.0 6.6 %copy.28 = f32[2,2,64,4096]{3,2,1,0:T(8,128)} copy(f32[2,2,64,4096]{3,1,0,2:T(2,128)} %all-to-all-done.1) | data formatting | bytes 8388608 | tf_op jit(solution)/shard_map/all_to_all | solution.py:100
  407.5 11.3 %scatter_custom_fusion = f32[512,4096]{1,0:T(8,128)} fusion(s32[256]{0:T(256)S(1)} %reshape.253, f32[256,4096]{1,0:T(8,128)} %bitcast.61, f32[]{:T(128)} %constant.159.clone.1), kind=kCustom, calls=%fused_computation.90 | custom fusion | flops 1048576 | bytes 8389120 | tf_op jit(solution)/shard_map/scatter-add | solution.py:102
  418.8 79.2 %reduce-scatter.2.cloned.1.call-done = f32[128,4096]{1,0:T(8,128)} async-done(((f32[512,4096]{1,0:T(8,128)}), f32[128,4096]{1,0:T(8,128)}) %reduce-scatter.2.cloned.1.call-update) | async-done | bytes 2097168 | tf_op jit(solution)/shard_map/reduce_scatter | solution.py:103
  (64 shorter events, 14.0 us)
Async XLA Ops:
  6.5 92.1 %all-gather.2.cloned.1.call-start = ((), (), s32[]{:S(2)}) async-start(), calls=%async_computation.3 | async-start | bytes 10485760 | tf_op jit(solution)/shard_map/all_gather | solution.py:83
  115.0 11.0 %copy-start.3 = (s32[512,3]{0,1:T(4,128)S(1)}, s32[512,3]{0,1:T(4,128)}, u32[]{:S(2)}) copy-start(s32[512,3]{0,1:T(4,128)} %param.6) | copy-start | bytes 18436
  115.0 106.9 %all-to-all-start = ((f32[2,2,64,4096]{3,1,0,2:T(2,128)}), f32[2,2,64,4096]{3,1,0,2:T(2,128)}, u32[]{:S(2)}, u32[]{:S(2)}) async-start(f32[2,2,64,4096]{3,1,0,2:T(2,128)} %copy.23), calls=%async_computation | async-start | bytes 8388608 | tf_op jit(solution)/shard_map/all_to_all | solution.py:87
  229.6 4.8 copy-start
  230.3 2.3 copy-start.1
  250.7 6.7 %copy-start.2 = (f32[1,1,64,4096]{3,2,1,0:T(8,128)S(1)}, f32[1,1,64,4096]{3,2,1,0:T(8,128)}, u32[]{:S(2)}) copy-start(f32[1,1,64,4096]{3,2,1,0:T(8,128)} %get-tuple-element.231) | copy-start | bytes 3145732 | tf_op jit(solution)/shard_map/while
  268.1 4.8 copy-start
  268.9 2.3 copy-start.1
  289.2 6.7 %copy-start.2 = (f32[1,1,64,4096]{3,2,1,0:T(8,128)S(1)}, f32[1,1,64,4096]{3,2,1,0:T(8,128)}, u32[]{:S(2)}) copy-start(f32[1,1,64,4096]{3,2,1,0:T(8,128)} %get-tuple-element.231) | copy-start | bytes 3145732 | tf_op jit(solution)/shard_map/while
  299.1 101.9 %all-to-all-start.1 = ((f32[2,2,64,4096]{3,1,0,2:T(2,128)}), f32[2,2,64,4096]{3,1,0,2:T(2,128)}, u32[]{:S(2)}, u32[]{:S(2)}) async-start(f32[2,2,64,4096]{3,1,0,2:T(2,128)} %get-tuple-element.107), calls=%async_computation.1 | async-start | bytes 8388608 | tf_op jit(solution)/shard_map/all_to_all | solution.py:100
  305.1 193.0 %reduce-scatter.2.cloned.1.call-start = ((), (), s32[]{:S(2)}) async-start(), calls=%async_computation.4 | async-start | bytes 10485760 | tf_op jit(solution)/shard_map/reduce_scatter | solution.py:103
Sparse Core Ops, SparseCore 0:
  9.2 89.4 all-gather.1
  419.0 79.0 reduce-scatter.1
where the time goes:
time: 506 us; the launch traced here: 505 us
  waiting for transfers between devices  358 us (71%)
  local copies, waits for them, and re-layouts  47.1 us (9%)
  other arithmetic  43.2 us (9%)
  loops' own time  24.6 us (5%)
  starting transfers between devices  17.1 us (3%)
  between operations  13.5 us (3%)
    all_to_all x1, waiting for transfers between devices, body(): lax.all_to_all(terms, 'grid', split_axis=2, concat_axis=2, tiled=True)  95.8 us
    all_to_all x1, waiting for transfers between devices, body(): lax.all_to_all(outgoing, 'grid', split_axis=2, concat_axis=2, tiled=True)  93.9 us
    all_gather x1, waiting for transfers between devices, body(): pieces = lax.all_gather(orbitals, 'grp', axis=0, tiled=True)  88.3 us
    reduce_scatter x1, waiting for transfers between devices, body(): return lax.psum_scatter(summed, 'grp', scatter_dimension=0, tiled=True)  79.2 us
    another operation x1, loops' own time, body(): terms = lax.map(solve_slot, (arrived, offsets, own_filled))  24.6 us
    gather x2, local copies, waits for them, and re-layouts, body(): outgoing = pieces[gather_ids]  16.4 us
    scatter-add x1, other arithmetic, body(): jax.ops.segment_sum(flat_terms, gather_ids.reshape(-1), num_segments=anch...  11.3 us
    all_to_all x1, starting transfers between devices, body(): lax.all_to_all(outgoing, 'grid', split_axis=2, concat_axis=2, tiled=True)  11 us
  transfers between devices with their start and end apart: 4, of which 4 were waited for; matrix products, arithmetic and copies ran while one was open for 1% of the time, Pallas kernels for 0%

commit v1 on v0

--- a/solution.py
+++ b/solution.py
@@ -6,6 +6,19 @@
 B = 64
 PAIR_DEV = 2
 ITERS = 3
+
+
+def collect(x, axis, dim):
+    ways = lax.axis_size(axis)
+    up = [(d, (d + 1) % ways) for d in range(ways)]
+    down = [(d, (d - 1) % ways) for d in range(ways)]
+    earlier, later = ([x], [x])
+    for _ in range(ways // 2):
+        earlier.append(lax.ppermute(earlier[-1], axis, up))
+    for _ in range((ways - 1) // 2):
+        later.append(lax.ppermute(later[-1], axis, down))
+    line = jnp.concatenate([*earlier[::-1], *later[1:]], axis=dim)
+    return jnp.roll(line, (lax.axis_index(axis) - ways // 2) * x.shape[dim], axis=dim)
 
 
 def shift_field(field, offset, extent):
@@ -80,7 +93,7 @@
     assignment = deal_evenly(pair_slots, owner_count, PAIR_DEV)
     filled = assignment[..., 0] >= 0
     safe_ids = jnp.maximum(assignment, 0)
-    pieces = lax.all_gather(orbitals, "grp", axis=0, tiled=True)
+    pieces = collect(orbitals, "grp", 0)
     group_table = lax.dynamic_slice_in_dim(safe_ids, group_idx * grid_count, grid_count, 0)
     gather_ids = jnp.transpose(group_table, (1, 2, 0))
     outgoing = pieces[gather_ids]

time: 506 us -> 526 us (1.040)
  starting transfers between devices: 17.1 us -> 29.1 us
  local copies, waits for them, and re-layouts: 47.1 us -> 58.6 us
  waiting for transfers between devices: 358 us -> 352 us
    all_gather x1 -> x0, waiting for transfers between devices: 88.3 us -> none  [body(): pieces = lax.all_gather(orbitals, 'grp', axis=0, tiled=True)]
    ppermute x0 -> x3, waiting for transfers between devices: none -> 84 us  [the longest x2 84 us: collect(): earlier.append(lax.ppermute(earlier[-1], axis, up))]
    all_to_all x1, starting transfers between devices: 11 us -> 17.1 us  [body(): lax.all_to_all(outgoing, 'grid', split_axis=2, concat_axis=2, tiled=True)]
    ppermute x0 -> x3, starting transfers between devices: none -> 5.93 us  [the longest x2 3.93 us: collect(): earlier.append(lax.ppermute(earlier[-1], axis, up))]
    unnamed x4 -> x13, local copies, waits for them, and re-layouts: 0.98 us -> 6.9 us
  transfers between devices with their start and end apart: 4 -> 6, of which waited for: 4 -> 5; matrix products, arithmetic and copies ran while one was open for 1% -> 1% of each run, Pallas kernels for 0% -> 0%
where the time goes in v1:
time: 526 us; the launch traced here: 523 us
  waiting for transfers between devices  352 us (67%)
  local copies, waits for them, and re-layouts  58.6 us (11%)
  other arithmetic  43.2 us (8%)
  starting transfers between devices  29.1 us (6%)
  loops' own time  25 us (5%)
  between operations  13.8 us (3%)
    all_to_all x1, waiting for transfers between devices, body(): lax.all_to_all(terms, 'grid', split_axis=2, concat_axis=2, tiled=True)  95.8 us
    all_to_all x1, waiting for transfers between devices, body(): lax.all_to_all(outgoing, 'grid', split_axis=2, concat_axis=2, tiled=True)  93.9 us
    ppermute x2, waiting for transfers between devices, collect(): earlier.append(lax.ppermute(earlier[-1], axis, up))  84 us
    reduce_scatter x1, waiting for transfers between devices, body(): return lax.psum_scatter(summed, 'grp', scatter_dimension=0, tiled=True)  78.1 us
    another operation x1, loops' own time, body(): terms = lax.map(solve_slot, (arrived, offsets, own_filled))  25 us
    all_to_all x1, starting transfers between devices, body(): lax.all_to_all(outgoing, 'grid', split_axis=2, concat_axis=2, tiled=True)  17.1 us
    gather x2, local copies, waits for them, and re-layouts, body(): outgoing = pieces[gather_ids]  16.4 us
    scatter-add x1, other arithmetic, body(): jax.ops.segment_sum(flat_terms, gather_ids.reshape(-1), num_segments=anch...  11.3 us
  transfers between devices with their start and end apart: 6, of which 5 were waited for; matrix products, arithmetic and copies ran while one was open for 1% of the time, Pallas kernels for 0%

profile of v1, /device:TPU:1, one launch (start us, length us, event | category | flops | bytes accessed | tf_op | source)
XLA Modules:
  0.0 522.9 jit_solution(15622221826311450193)
XLA Ops:
  6.5 2.0 collective-permute-start
  8.6 44.5 %collective-permute-done = f32[128,4096]{1,0:T(8,128)S(1)} collective-permute-done((f32[128,4096]{1,0:T(8,128)}, f32[128,4096]{1,0:T(8,128)S(1)}, u32[]{:S(2)}, u32[]{:S(2)}) %collective-permute-start) | collective-permute-done | bytes 2097184 | tf_op jit(solution)/shard_map/ppermute | solution.py:17
  53.1 1.9 collective-permute-start.1
  55.0 2.0 collective-permute-start.2
  60.1 39.5 %collective-permute-done.1 = f32[128,4096]{1,0:T(8,128)} collective-permute-done((f32[128,4096]{1,0:T(8,128)S(1)}, f32[128,4096]{1,0:T(8,128)}, u32[]{:S(2)}, u32[]{:S(2)}) %collective-permute-start.1) | collective-permute-done | bytes 2097184 | tf_op jit(solution)/shard_map/ppermute | solution.py:17
  99.6 1.7 constant_dynamic-update-slice_fusion.7
  101.7 1.7 constant_dynamic-update-slice_fusion.4
  103.4 1.7 constant_dynamic-update-slice_fusion.3
  105.5 1.7 constant_dynamic-update-slice_fusion
  107.3 3.8 constant_dynamic-slice_fusion.3
  111.1 9.0 %gather_fusion = f32[256,4096]{1,0:T(8,128)} fusion(f32[512,4096]{1,0:T(8,128)} %constant_dynamic-slice_fusion.3, s32[1024]{0:T(1024)S(1)} %pad_clamp_fusion.2), kind=kCustom, calls=%fused_computation | custom fusion | bytes 8389632 | tf_op jit(solution)/shard_map/gather | solution.py:99
  120.1 7.4 %copy.23 = f32[2,2,64,4096]{3,1,0,2:T(2,128)} copy(f32[2,2,64,4096]{3,2,1,0:T(8,128)} %bitcast.60) | data formatting | bytes 8388608 | tf_op jit(solution)/shard_map/gather | solution.py:99
  127.5 17.1 %all-to-all-start = ((f32[2,2,64,4096]{3,1,0,2:T(2,128)}), f32[2,2,64,4096]{3,1,0,2:T(2,128)}, u32[]{:S(2)}, u32[]{:S(2)}) async-start(f32[2,2,64,4096]{3,1,0,2:T(2,128)} %copy.23), calls=%async_computation | async-start | bytes 8388608 | tf_op jit(solution)/shard_map/all_to_all | solution.py:100
  146.5 93.9 %all-to-all-done = f32[2,2,64,4096]{3,1,0,2:T(2,128)} async-done(((f32[2,2,64,4096]{3,1,0,2:T(2,128)}), f32[2,2,64,4096]{3,1,0,2:T(2,128)}, u32[]{:S(2)}, u32[]{:S(2)}) %all-to-all-start) | async-done | bytes 4194336 | tf_op jit(solution)/shard_map/all_to_all | solution.py:100
  240.5 77.5 %while.13 = (s32[]{:T(128)}, f32[2,2,64,4096]{3,1,0,2:T(2,128)}, f32[2,2,64,4096]{3,1,0,2:T(2,128)}, s32[2,3]{1,0:T(2,128)S(1)}, pred[2]{0:T(512)(128)(4,1)S(1)}...) while((s32[]{:T(128)}, f32[2,2,64,4096]{3,1,0,2:T(2,128)}, ...), condition=%wide.region_8.9_spmd, body=%wide.region_1.8_spmd.sunk | while | flops 22224920 | bytes 64017664 | solution.py:112
  243.8 4.4 constant_dynamic-slice_fusion.6
  251.3 1.8 multiply_reduce_fusion.9
  256.7 1.8 multiply_reduce_fusion.11
  262.3 1.8 fusion.79
  265.4 3.9 multiply_bitcast_fusion.2
  276.2 3.0 copy_dynamic-update-slice_fusion.2
  282.4 4.4 constant_dynamic-slice_fusion.6
  289.8 1.8 multiply_reduce_fusion.9
  295.3 1.8 multiply_reduce_fusion.11
  300.9 1.8 fusion.79
  303.9 3.9 multiply_bitcast_fusion.2
  314.8 3.0 copy_dynamic-update-slice_fusion.2
  317.9 6.0 %all-to-all-start.1 = ((f32[2,2,64,4096]{3,1,0,2:T(2,128)}), f32[2,2,64,4096]{3,1,0,2:T(2,128)}, u32[]{:S(2)}, u32[]{:S(2)}) async-start(f32[2,2,64,4096]{3,1,0,2:T(2,128)} %get-tuple-element.107), calls=%async_computation.1 | async-start | bytes 8388608 | tf_op jit(solution)/shard_map/all_to_all | solution.py:113
  324.1 95.8 %all-to-all-done.1 = f32[2,2,64,4096]{3,1,0,2:T(2,128)} async-done(((f32[2,2,64,4096]{3,1,0,2:T(2,128)}), f32[2,2,64,4096]{3,1,0,2:T(2,128)}, u32[]{:S(2)}, u32[]{:S(2)}) %all-to-all-start.1) | async-done | bytes 4194336 | tf_op jit(solution)/shard_map/all_to_all | solution.py:113
  419.9 6.6 %copy.28 = f32[2,2,64,4096]{3,2,1,0:T(8,128)} copy(f32[2,2,64,4096]{3,1,0,2:T(2,128)} %all-to-all-done.1) | data formatting | bytes 8388608 | tf_op jit(solution)/shard_map/all_to_all | solution.py:113
  426.4 11.3 %scatter_custom_fusion = f32[512,4096]{1,0:T(8,128)} fusion(s32[256]{0:T(256)S(1)} %reshape.253, f32[256,4096]{1,0:T(8,128)} %bitcast.61, f32[]{:T(128)} %constant.180.clone.1), kind=kCustom, calls=%fused_computation.90 | custom fusion | flops 1048576 | bytes 8389120 | tf_op jit(solution)/shard_map/scatter-add | solution.py:115
  437.7 78.1 %reduce-scatter.2.cloned.1.call-done = f32[128,4096]{1,0:T(8,128)} async-done(((f32[512,4096]{1,0:T(8,128)}), f32[128,4096]{1,0:T(8,128)}) %reduce-scatter.2.cloned.1.call-update) | async-done | bytes 2097168 | tf_op jit(solution)/shard_map/reduce_scatter | solution.py:116
  (78 shorter events, 24.9 us)
Async XLA Ops:
  6.5 46.6 %collective-permute-start = (f32[128,4096]{1,0:T(8,128)}, f32[128,4096]{1,0:T(8,128)S(1)}, u32[]{:S(2)}, u32[]{:S(2)}) collective-permute-start(f32[128,4096]{1,0:T(8,128)} %param.5), channel_id=1, source_target_pairs={{0,64},{64,128},{128,192},{192,0},{1,65},{65,129},{129,193},{193,1... | collective-permute-start | bytes 6291464 | tf_op jit(solution)/shard_map/ppermute | solution.py:17
  53.1 46.5 %collective-permute-start.1 = (f32[128,4096]{1,0:T(8,128)S(1)}, f32[128,4096]{1,0:T(8,128)}, u32[]{:S(2)}, u32[]{:S(2)}) collective-permute-start(f32[128,4096]{1,0:T(8,128)S(1)} %collective-permute-done), channel_id=1, source_target_pairs={{0,64},{64,128},{128,192},{192,0},{1,65},{65,129},{129,193},{193,1... | collective-permute-start | bytes 6291464 | tf_op jit(solution)/shard_map/ppermute | solution.py:17
  55.0 46.7 %collective-permute-start.2 = (f32[128,4096]{1,0:T(8,128)}, f32[128,4096]{1,0:T(8,128)}, u32[]{:S(2)}, u32[]{:S(2)}) collective-permute-start(f32[128,4096]{1,0:T(8,128)} %param.5), channel_id=1, source_target_pairs={{0,192},{64,0},{128,64},{192,128},{1,193},{65,1},{129,65},{193,129... | collective-permute-start | bytes 6291464 | tf_op jit(solution)/shard_map/ppermute | solution.py:19
  60.1 41.4 %copy-start.3 = (f32[128,4096]{1,0:T(8,128)S(1)}, f32[128,4096]{1,0:T(8,128)}, u32[]{:S(2)}) copy-start(f32[128,4096]{1,0:T(8,128)} %param.5) | copy-start | bytes 6291460
  127.5 17.1 %copy-start.4 = (s32[512,3]{0,1:T(4,128)S(1)}, s32[512,3]{0,1:T(4,128)}, u32[]{:S(2)}) copy-start(s32[512,3]{0,1:T(4,128)} %param.6) | copy-start | bytes 18436
  127.5 113.0 %all-to-all-start = ((f32[2,2,64,4096]{3,1,0,2:T(2,128)}), f32[2,2,64,4096]{3,1,0,2:T(2,128)}, u32[]{:S(2)}, u32[]{:S(2)}) async-start(f32[2,2,64,4096]{3,1,0,2:T(2,128)} %copy.23), calls=%async_computation | async-start | bytes 8388608 | tf_op jit(solution)/shard_map/all_to_all | solution.py:100
  248.2 4.8 copy-start
  249.0 2.3 copy-start.1
  269.3 6.7 %copy-start.2 = (f32[1,1,64,4096]{3,2,1,0:T(8,128)S(1)}, f32[1,1,64,4096]{3,2,1,0:T(8,128)}, u32[]{:S(2)}) copy-start(f32[1,1,64,4096]{3,2,1,0:T(8,128)} %get-tuple-element.231) | copy-start | bytes 3145732 | tf_op jit(solution)/shard_map/while
  286.8 4.8 copy-start
  287.6 2.3 copy-start.1
  307.8 6.7 %copy-start.2 = (f32[1,1,64,4096]{3,2,1,0:T(8,128)S(1)}, f32[1,1,64,4096]{3,2,1,0:T(8,128)}, u32[]{:S(2)}) copy-start(f32[1,1,64,4096]{3,2,1,0:T(8,128)} %get-tuple-element.231) | copy-start | bytes 3145732 | tf_op jit(solution)/shard_map/while
  317.9 101.9 %all-to-all-start.1 = ((f32[2,2,64,4096]{3,1,0,2:T(2,128)}), f32[2,2,64,4096]{3,1,0,2:T(2,128)}, u32[]{:S(2)}, u32[]{:S(2)}) async-start(f32[2,2,64,4096]{3,1,0,2:T(2,128)} %get-tuple-element.107), calls=%async_computation.1 | async-start | bytes 8388608 | tf_op jit(solution)/shard_map/all_to_all | solution.py:113
  324.0 191.8 %reduce-scatter.2.cloned.1.call-start = ((), (), s32[]{:S(2)}) async-start(), calls=%async_computation.3 | async-start | bytes 10485760 | tf_op jit(solution)/shard_map/reduce_scatter | solution.py:116
Sparse Core Ops, SparseCore 0:
  437.8 77.9 reduce-scatter.1
